TPU v7x, 32 devices: a whole 2x2x4 slice. The times are simulated.
32 devices in a mesh: row: 4 (over x, core), col: 4 (over z), layer: 2 (over y).
Axes of the slice: x: 2, y: 2, z: 4, core: 2. Of those that a mesh axis runs over, the one named last changes fastest.
Arguments:
- a_vals: bfloat16 [4, 4, 2, 24, 128, 128], P('row', 'col', 'layer'), may hold values from -1.1953125 to 1.1953125
- a_pos: int32 [4, 4, 2, 24], P('row', 'col', 'layer'), may hold values from 0 to 31, as said below
- a_count: int32 [4, 4, 2], P('row', 'col', 'layer'), may hold values from 6 to 24
- b_vals: bfloat16 [4, 4, 2, 1, 6, 128, 128], P('row', 'col', 'layer'), may hold values from -1.1953125 to 1.1953125
- b_pos: int32 [4, 4, 2, 1, 6], P('row', 'col', 'layer'), may hold values from 0 to 31, as said below
- b_count: int32 [4, 4, 2, 1], P('row', 'col', 'layer'), may hold values from 1 to 6
Outputs:
- product: float32 [4096, 4096], P('row', ('col', 'layer'))
Inputs may be any that keep to these rules, and one draw needn't show every extreme that they name: `a_pos`: within one panel (fixed first three indices) the 24 entries are distinct. `b_pos`: within one panel (fixed first four indices) the 6 entries are distinct.
All inputs are finite; a program needn't handle non-finite values.
Results may differ from a plain program's by a relative error of at most 0.0003.
Values may be sent and summed in bfloat16 or wider, within the bound.
A program may use at most 64 MiB of HBM per device.

v0:
```python
import jax
import jax.numpy as jnp
from jax import lax
from jax.sharding import PartitionSpec as P

KB = 4
CB = 8
RB = 8


def passed_along(block, axis, distance):
    devices = range(lax.axis_size(axis))
    route = [((i - distance) % len(devices), i) for i in devices]
    return lax.ppermute(block, axis, route)


def contribute(total, a_vals, a_pos, a_count, b_vals, b_pos, b_count):
    block = a_vals.shape[-1]
    slots_a = a_vals.shape[0]
    target = a_pos % KB * RB + a_pos // KB
    live_a = jnp.arange(slots_a, dtype=jnp.int32) < a_count
    places = jnp.arange(KB * RB, dtype=jnp.int32)
    select = ((target[:, None] == places[None, :]) & live_a[:, None]).astype(jnp.bfloat16)
    placed = jnp.einsum("sp,sab->pab", select, a_vals, preferred_element_type=jnp.float32).astype(
        jnp.bfloat16
    )
    columns = placed.reshape(KB, RB * block, block)
    for slot in range(b_vals.shape[0]):
        entry = b_pos[slot]
        left = lax.dynamic_index_in_dim(columns, entry // CB, 0, keepdims=False)
        term = jnp.dot(left, b_vals[slot], preferred_element_type=jnp.float32)
        live = (slot < b_count).astype(jnp.float32)
        start = entry % CB * block
        old = lax.dynamic_slice_in_dim(total, start, block, 1)
        total = lax.dynamic_update_slice_in_dim(total, old + live * term, start, 1)
    return total


def pick(state, index):
    return tuple((lax.dynamic_index_in_dim(member, index, 0, keepdims=False) for member in state))


def per_device(a_vals, a_pos, a_count, b_vals, b_pos, b_count):
    n_row = lax.axis_size("row")
    n_col = lax.axis_size("col")
    row_i = lax.axis_index("row")
    col_j = lax.axis_index("col")
    block = a_vals.shape[-1]
    a_state = (a_vals[0, 0], a_pos[0, 0], a_count[0, 0])
    b_state = (b_vals[0, 0, 0], b_pos[0, 0, 0], b_count[0, 0, 0])

    def apply(total, a_now, b_now, turn):
        wanted = (row_i + col_j + turn) % n_col
        a_index = 0
        b_index = wanted // n_row
        a_part = pick(a_now, a_index)
        b_part = pick(b_now, b_index)
        return contribute(total, a_part[0], a_part[1], a_part[2], b_part[0], b_part[1], b_part[2])

    def advance(turn, carry):
        total, a_now, b_now = carry
        total = apply(total, a_now, b_now, turn)
        a_now = passed_along((a_now[0], a_now[1], a_now[2]), "col", -1)
        b_now = passed_along((b_now[0], b_now[1], b_now[2]), "row", -1)
        return (total, tuple(a_now), tuple(b_now))

    start = jnp.zeros((RB * block, CB * block), jnp.float32)
    total, a_now, b_now = lax.fori_loop(
        0, n_col - 1, advance, (start, tuple(a_state), tuple(b_state))
    )
    total = apply(total, a_now, b_now, n_col - 1)
    return lax.psum_scatter(total, "layer", scatter_dimension=1, tiled=True)


def solution(mesh):
    placed = (
        P("row", "col", "layer", None, None, None),
        P("row", "col", "layer", None),
        P("row", "col", "layer"),
        P("row", "col", "layer", None, None, None, None),
        P("row", "col", "layer", None, None),
        P("row", "col", "layer", None),
    )
    return jax.shard_map(
        per_device,
        mesh=mesh,
        in_specs=placed,
        out_specs=P("row", ("col", "layer")),
        check_vma=False,
    )
```

profile of v0, /device:TPU:0, one launch (start us, length us, event | category | flops | bytes accessed | tf_op | source)
XLA Modules:
  0.0 265.2 jit_solution(10245264982379443777)
XLA Ops:
  6.5 1.7 copy.12
  9.5 2.5 broadcast_in_dim.15
  12.0 161.7 %while.25 = (s32[]{:T(128)}, f32[1024,1024]{1,0:T(8,128)}, bf16[1,24,128,128]{3,1,2,0:T(8,128)(2,1)S(1)}, s32[1,24]{1,0:T(1,128)S(1)}, s32[1]{0:T(128)}, /*index...) while((s32[]{:T(128)}, f32[1024,1024]{1,0:T(8,128)}, ...), condition=%wide.region_1.2_spmd, body=%wide.region_0.1_spmd.sunk | while | flops 228591648 | bytes 17897736 | solution.py:68
  12.0 2.4 collective-permute-start.3
  14.5 3.2 %collective-permute-start.5 = (s32[1]{0:T(128)}, s32[1]{0:T(128)}, u32[]{:S(2)}, u32[]{:S(2)}) collective-permute-start(s32[1]{0:T(128)} %copy.36), channel_id=1, source_target_pairs={{8,0},{16,8},{24,16},{0,24},{9,1},{17,9},{25,17},{1,25},{10,2},{18... | collective-permute-start | bytes 20 | tf_op jit(solution)/shard_map/while/body/eval_jaxpr/ppermute | solution.py:14
  17.8 3.7 %collective-permute-start = (bf16[1,24,128,128]{3,1,2,0:T(8,128)(2,1)S(1)}, bf16[1,24,128,128]{3,1,2,0:T(8,128)(2,1)S(1)}, u32[]{:S(2)}, u32[]{:S(2)}) collective-permute-start(bf16[1,24,128,128]{3,1,2,0:T(8,128)(2,1)S(1)} %copy.31), channel_id=1, source_target_pairs={{2,0},{4,2},{6,4},{0,6},{3,1},{5,3},{7,5},{1,7},{10,8},{12,10},{14... | collective-permute-start | bytes 2359304 | tf_op jit(solution)/shard_map/while/body/eval_jaxpr/ppermute | solution.py:14
  21.9 14.7 %collective-permute-start.2 = (s32[1]{0:T(128)}, s32[1]{0:T(128)}, u32[]{:S(2)}, u32[]{:S(2)}) collective-permute-start(s32[1]{0:T(128)} %copy.33), channel_id=1, source_target_pairs={{2,0},{4,2},{6,4},{0,6},{3,1},{5,3},{7,5},{1,7},{10,8},{12,10},{14... | collective-permute-start | bytes 20 | tf_op jit(solution)/shard_map/while/body/eval_jaxpr/ppermute | solution.py:14
  36.6 0.7 fusion.138
  45.0 0.5 convolution_convert_fusion.3
  46.0 2.1 fusion.140
  48.0 2.1 fusion.141
  50.1 2.1 fusion.142
  59.6 2.1 fusion.143
  61.7 2.1 fusion.144
  63.8 2.1 fusion.145
  65.9 1.3 collective-permute-done.4
  68.5 1.7 collective-permute-start.3
  70.2 3.2 %collective-permute-start.5 = (s32[1]{0:T(128)}, s32[1]{0:T(128)}, u32[]{:S(2)}, u32[]{:S(2)}) collective-permute-start(s32[1]{0:T(128)} %copy.36), channel_id=1, source_target_pairs={{8,0},{16,8},{24,16},{0,24},{9,1},{17,9},{25,17},{1,25},{10,2},{18... | collective-permute-start | bytes 20 | tf_op jit(solution)/shard_map/while/body/eval_jaxpr/ppermute | solution.py:14
  73.5 0.6 collective-permute-start
  74.6 14.7 %collective-permute-start.2 = (s32[1]{0:T(128)}, s32[1]{0:T(128)}, u32[]{:S(2)}, u32[]{:S(2)}) collective-permute-start(s32[1]{0:T(128)} %copy.33), channel_id=1, source_target_pairs={{2,0},{4,2},{6,4},{0,6},{3,1},{5,3},{7,5},{1,7},{10,8},{12,10},{14... | collective-permute-start | bytes 20 | tf_op jit(solution)/shard_map/while/body/eval_jaxpr/ppermute | solution.py:14
  89.2 0.7 fusion.138
  97.6 0.5 convolution_convert_fusion.3
  98.6 2.1 fusion.140
  100.7 2.1 fusion.141
  102.8 2.1 fusion.142
  112.2 2.1 fusion.143
  114.3 2.1 fusion.144
  116.4 2.1 fusion.145
  118.4 1.3 collective-permute-done.4
  121.1 1.7 collective-permute-start.3
  122.8 3.2 %collective-permute-start.5 = (s32[1]{0:T(128)}, s32[1]{0:T(128)}, u32[]{:S(2)}, u32[]{:S(2)}) collective-permute-start(s32[1]{0:T(128)} %copy.36), channel_id=1, source_target_pairs={{8,0},{16,8},{24,16},{0,24},{9,1},{17,9},{25,17},{1,25},{10,2},{18... | collective-permute-start | bytes 20 | tf_op jit(solution)/shard_map/while/body/eval_jaxpr/ppermute | solution.py:14
  127.2 14.6 %collective-permute-start.2 = (s32[1]{0:T(128)}, s32[1]{0:T(128)}, u32[]{:S(2)}, u32[]{:S(2)}) collective-permute-start(s32[1]{0:T(128)} %copy.33), channel_id=1, source_target_pairs={{2,0},{4,2},{6,4},{0,6},{3,1},{5,3},{7,5},{1,7},{10,8},{12,10},{14... | collective-permute-start | bytes 20 | tf_op jit(solution)/shard_map/while/body/eval_jaxpr/ppermute | solution.py:14
  141.8 0.7 fusion.138
  151.2 2.1 fusion.140
  153.3 2.1 fusion.141
  155.4 2.1 fusion.142
  164.8 2.1 fusion.143
  166.9 2.1 fusion.144
  169.0 2.1 fusion.145
  171.1 1.3 collective-permute-done.4
  173.7 0.7 fusion.101
  191.0 2.1 fusion.51
  193.0 2.1 fusion.53
  195.1 2.1 fusion.55
  197.2 2.1 fusion.57
  199.3 2.1 fusion.59
  201.4 2.1 fusion.61
  203.5 54.9 %reduce-scatter.2.cloned.1.call-done = f32[1024,512]{1,0:T(8,128)} async-done(((f32[1024,1024]{1,0:T(8,128)}), f32[1024,512]{1,0:T(8,128)}) %reduce-scatter.2.cloned.1.call-update) | async-done | bytes 2097168 | tf_op jit(solution)/shard_map/reduce_scatter | solution.py:72
  (56 shorter events, 5.1 us)
Async XLA Ops:
  6.5 5.5 %copy-start.2 = (s32[1,1,1,24]{3,2,1,0:T(1,128)S(1)}, s32[1,1,1,24]{3,2,1,0:T(1,128)}, u32[]{:S(2)}) copy-start(s32[1,1,1,24]{3,2,1,0:T(1,128)} %param.9) | copy-start | bytes 292
  6.5 5.5 %copy-start = (bf16[1,1,1,1,6,128,128]{6,5,4,3,2,1,0:T(8,128)(2,1)S(1)}, bf16[1,1,1,1,6,128,128]{6,5,4,3,2,1,0:T(8,128)(2,1)}, u32[]{:S(2)}) copy-start(bf16[1,1,1,1,6,128,128]{6,5,4,3,2,1,0:T(8,128)(2,1)} %param.11) | copy-start | bytes 589828
  6.5 5.5 %copy-start.1 = (s32[1,1,1,1,6]{4,3,2,1,0:T(1,128)S(1)}, s32[1,1,1,1,6]{4,3,2,1,0:T(1,128)}, u32[]{:S(2)}) copy-start(s32[1,1,1,1,6]{4,3,2,1,0:T(1,128)} %param.12) | copy-start | bytes 76
  6.5 251.9 %reduce-scatter.2.cloned.1.call-start = ((), (), s32[]{:S(2)}) async-start(), calls=%async_computation.1 | async-start | bytes 6291456 | tf_op jit(solution)/shard_map/reduce_scatter | solution.py:72
  12.0 55.1 %collective-permute-start.3 = (bf16[1,6,128,128]{3,2,1,0:T(8,128)(2,1)S(1)}, bf16[1,6,128,128]{3,2,1,0:T(8,128)(2,1)S(1)}, u32[]{:S(2)}, u32[]{:S(2)}) collective-permute-start(bf16[1,6,128,128]{3,2,1,0:T(8,128)(2,1)S(1)} %copy.34), channel_id=1, source_target_pairs={{8,0},{16,8},{24,16},{0,24},{9,1},{17,9},{25,17},{1,25},{10,2},{18... | collective-permute-start | bytes 589832 | tf_op jit(solution)/shard_map/while/body/eval_jaxpr/ppermute | solution.py:14
  14.5 51.4 %collective-permute-start.5 = (s32[1]{0:T(128)}, s32[1]{0:T(128)}, u32[]{:S(2)}, u32[]{:S(2)}) collective-permute-start(s32[1]{0:T(128)} %copy.36), channel_id=1, source_target_pairs={{8,0},{16,8},{24,16},{0,24},{9,1},{17,9},{25,17},{1,25},{10,2},{18... | collective-permute-start | bytes 20 | tf_op jit(solution)/shard_map/while/body/eval_jaxpr/ppermute | solution.py:14
  17.8 49.4 %collective-permute-start = (bf16[1,24,128,128]{3,1,2,0:T(8,128)(2,1)S(1)}, bf16[1,24,128,128]{3,1,2,0:T(8,128)(2,1)S(1)}, u32[]{:S(2)}, u32[]{:S(2)}) collective-permute-start(bf16[1,24,128,128]{3,1,2,0:T(8,128)(2,1)S(1)} %copy.31), channel_id=1, source_target_pairs={{2,0},{4,2},{6,4},{0,6},{3,1},{5,3},{7,5},{1,7},{10,8},{12,10},{14... | collective-permute-start | bytes 2359304 | tf_op jit(solution)/shard_map/while/body/eval_jaxpr/ppermute | solution.py:14
  21.4 45.7 %collective-permute-start.1 = (s32[1,24]{1,0:T(1,128)S(1)}, s32[1,24]{1,0:T(1,128)S(1)}, u32[]{:S(2)}, u32[]{:S(2)}) collective-permute-start(s32[1,24]{1,0:T(1,128)S(1)} %copy.32), channel_id=1, source_target_pairs={{2,0},{4,2},{6,4},{0,6},{3,1},{5,3},{7,5},{1,7},{10,8},{12,10},{14... | collective-permute-start | bytes 296 | tf_op jit(solution)/shard_map/while/body/eval_jaxpr/ppermute | solution.py:14
  21.9 44.0 %collective-permute-start.2 = (s32[1]{0:T(128)}, s32[1]{0:T(128)}, u32[]{:S(2)}, u32[]{:S(2)}) collective-permute-start(s32[1]{0:T(128)} %copy.33), channel_id=1, source_target_pairs={{2,0},{4,2},{6,4},{0,6},{3,1},{5,3},{7,5},{1,7},{10,8},{12,10},{14... | collective-permute-start | bytes 20 | tf_op jit(solution)/shard_map/while/body/eval_jaxpr/ppermute | solution.py:14
  65.9 1.3 collective-permute-start.4
  68.5 51.2 %collective-permute-start.3 = (bf16[1,6,128,128]{3,2,1,0:T(8,128)(2,1)S(1)}, bf16[1,6,128,128]{3,2,1,0:T(8,128)(2,1)S(1)}, u32[]{:S(2)}, u32[]{:S(2)}) collective-permute-start(bf16[1,6,128,128]{3,2,1,0:T(8,128)(2,1)S(1)} %copy.34), channel_id=1, source_target_pairs={{8,0},{16,8},{24,16},{0,24},{9,1},{17,9},{25,17},{1,25},{10,2},{18... | collective-permute-start | bytes 589832 | tf_op jit(solution)/shard_map/while/body/eval_jaxpr/ppermute | solution.py:14
  70.2 48.2 %collective-permute-start.5 = (s32[1]{0:T(128)}, s32[1]{0:T(128)}, u32[]{:S(2)}, u32[]{:S(2)}) collective-permute-start(s32[1]{0:T(128)} %copy.36), channel_id=1, source_target_pairs={{8,0},{16,8},{24,16},{0,24},{9,1},{17,9},{25,17},{1,25},{10,2},{18... | collective-permute-start | bytes 20 | tf_op jit(solution)/shard_map/while/body/eval_jaxpr/ppermute | solution.py:14
  73.5 46.2 %collective-permute-start = (bf16[1,24,128,128]{3,1,2,0:T(8,128)(2,1)S(1)}, bf16[1,24,128,128]{3,1,2,0:T(8,128)(2,1)S(1)}, u32[]{:S(2)}, u32[]{:S(2)}) collective-permute-start(bf16[1,24,128,128]{3,1,2,0:T(8,128)(2,1)S(1)} %copy.31), channel_id=1, source_target_pairs={{2,0},{4,2},{6,4},{0,6},{3,1},{5,3},{7,5},{1,7},{10,8},{12,10},{14... | collective-permute-start | bytes 2359304 | tf_op jit(solution)/shard_map/while/body/eval_jaxpr/ppermute | solution.py:14
  74.1 45.6 %collective-permute-start.1 = (s32[1,24]{1,0:T(1,128)S(1)}, s32[1,24]{1,0:T(1,128)S(1)}, u32[]{:S(2)}, u32[]{:S(2)}) collective-permute-start(s32[1,24]{1,0:T(1,128)S(1)} %copy.32), channel_id=1, source_target_pairs={{2,0},{4,2},{6,4},{0,6},{3,1},{5,3},{7,5},{1,7},{10,8},{12,10},{14... | collective-permute-start | bytes 296 | tf_op jit(solution)/shard_map/while/body/eval_jaxpr/ppermute | solution.py:14
  74.6 43.9 %collective-permute-start.2 = (s32[1]{0:T(128)}, s32[1]{0:T(128)}, u32[]{:S(2)}, u32[]{:S(2)}) collective-permute-start(s32[1]{0:T(128)} %copy.33), channel_id=1, source_target_pairs={{2,0},{4,2},{6,4},{0,6},{3,1},{5,3},{7,5},{1,7},{10,8},{12,10},{14... | collective-permute-start | bytes 20 | tf_op jit(solution)/shard_map/while/body/eval_jaxpr/ppermute | solution.py:14
  118.4 1.3 collective-permute-start.4
  121.1 51.3 %collective-permute-start.3 = (bf16[1,6,128,128]{3,2,1,0:T(8,128)(2,1)S(1)}, bf16[1,6,128,128]{3,2,1,0:T(8,128)(2,1)S(1)}, u32[]{:S(2)}, u32[]{:S(2)}) collective-permute-start(bf16[1,6,128,128]{3,2,1,0:T(8,128)(2,1)S(1)} %copy.34), channel_id=1, source_target_pairs={{8,0},{16,8},{24,16},{0,24},{9,1},{17,9},{25,17},{1,25},{10,2},{18... | collective-permute-start | bytes 589832 | tf_op jit(solution)/shard_map/while/body/eval_jaxpr/ppermute | solution.py:14
  122.8 48.2 %collective-permute-start.5 = (s32[1]{0:T(128)}, s32[1]{0:T(128)}, u32[]{:S(2)}, u32[]{:S(2)}) collective-permute-start(s32[1]{0:T(128)} %copy.36), channel_id=1, source_target_pairs={{8,0},{16,8},{24,16},{0,24},{9,1},{17,9},{25,17},{1,25},{10,2},{18... | collective-permute-start | bytes 20 | tf_op jit(solution)/shard_map/while/body/eval_jaxpr/ppermute | solution.py:14
  126.1 46.2 %collective-permute-start = (bf16[1,24,128,128]{3,1,2,0:T(8,128)(2,1)S(1)}, bf16[1,24,128,128]{3,1,2,0:T(8,128)(2,1)S(1)}, u32[]{:S(2)}, u32[]{:S(2)}) collective-permute-start(bf16[1,24,128,128]{3,1,2,0:T(8,128)(2,1)S(1)} %copy.31), channel_id=1, source_target_pairs={{2,0},{4,2},{6,4},{0,6},{3,1},{5,3},{7,5},{1,7},{10,8},{12,10},{14... | collective-permute-start | bytes 2359304 | tf_op jit(solution)/shard_map/while/body/eval_jaxpr/ppermute | solution.py:14
  126.7 45.7 %collective-permute-start.1 = (s32[1,24]{1,0:T(1,128)S(1)}, s32[1,24]{1,0:T(1,128)S(1)}, u32[]{:S(2)}, u32[]{:S(2)}) collective-permute-start(s32[1,24]{1,0:T(1,128)S(1)} %copy.32), channel_id=1, source_target_pairs={{2,0},{4,2},{6,4},{0,6},{3,1},{5,3},{7,5},{1,7},{10,8},{12,10},{14... | collective-permute-start | bytes 296 | tf_op jit(solution)/shard_map/while/body/eval_jaxpr/ppermute | solution.py:14
  127.2 43.9 %collective-permute-start.2 = (s32[1]{0:T(128)}, s32[1]{0:T(128)}, u32[]{:S(2)}, u32[]{:S(2)}) collective-permute-start(s32[1]{0:T(128)} %copy.33), channel_id=1, source_target_pairs={{2,0},{4,2},{6,4},{0,6},{3,1},{5,3},{7,5},{1,7},{10,8},{12,10},{14... | collective-permute-start | bytes 20 | tf_op jit(solution)/shard_map/while/body/eval_jaxpr/ppermute | solution.py:14
  171.1 1.3 collective-permute-start.4
Sparse Core Ops, SparseCore 0:
  203.7 54.7 reduce-scatter.1
where the time goes:
time: 267 us; the launch traced here: 265 us
  starting transfers between devices  65.7 us (25%)
  waiting for transfers between devices  58.8 us (22%)
  matrix products  52.3 us (20%)
  loops' own time  49.3 us (18%)
  between operations  30.3 us (11%)
  local copies, waits for them, and re-layouts  8.81 us (3%)
    ppermute x18, starting transfers between devices, passed_along(): return lax.ppermute(block, axis, route)  65.7 us
    reduce_scatter x1, waiting for transfers between devices, per_device(): return lax.psum_scatter(total, 'layer', scatter_dimension=1, tiled=True)  54.9 us
    dot_general x24, matrix products, contribute(): term = jnp.dot(left, b_vals[slot], preferred_element_type=jnp.float32)  50.1 us
    another operation x1, loops' own time, per_device(): lax.fori_loop(0, n_col - 1, advance, (start, tuple(a_state), tuple(b_stat...  49.3 us
  transfers between devices with their start and end apart: 19, of which 4 were waited for; matrix products, arithmetic and copies ran while one was open for 16% of the time, Pallas kernels for 0%

commit v1 on v0

v1 whole, which is shorter than its diff:
```python
import functools

import jax
import jax.numpy as jnp
from jax import lax
from jax.experimental import pallas as pl
from jax.experimental.pallas import tpu as pltpu
from jax.sharding import PartitionSpec as P

KB = 4
CB = 8
RB = 8
MESH = pl.DeviceIdType.MESH


def gather_kernel(
    n_row, n_col, n_layer, pieces,
    a_ref, am_ref, b_ref, bm_ref,
    a_all, am_all, b_all, bm_all,
    up_sem, down_sem, over_sem, a_recv, am_send, am_recv,
    b_send, b_pass, b_recv, bm_send, bm_recv, own_sem,
):
    i = lax.axis_index("row")
    c = lax.axis_index("col")
    l = lax.axis_index("layer")
    m = 1 - l
    size = a_ref.shape[0] // pieces
    half = pieces // 2
    short_cuts = n_col >= 4

    peers = []
    for dl in range(n_layer):
        ll = lax.rem(l + dl, n_layer)
        for dc in range(n_col):
            if dl or dc:
                peers.append((i, lax.rem(c + dc, n_col), ll))
    sides = []
    for dl in range(n_layer):
        ll = lax.rem(l + dl, n_layer)
        for dr in range(n_row):
            if dl or dr:
                sides.append((lax.rem(i + dr, n_row), c, ll))
    greeted = peers + [s for k, s in enumerate(sides) if (k + 1) % n_row != 0]

    barrier = pltpu.get_barrier_semaphore()
    for one in greeted:
        pl.semaphore_signal(barrier, inc=1, device_id=one, device_id_type=MESH)
    pl.semaphore_wait(barrier, len(greeted))

    sent = []

    def send(src, dst, s_sem, r_sem, to, when=None):
        def copy():
            return pltpu.make_async_remote_copy(
                src_ref=src, dst_ref=dst, send_sem=s_sem, recv_sem=r_sem,
                device_id=to, device_id_type=MESH)

        if when is None:
            copy().start()
        else:
            pl.when(when)(lambda: copy().start())
        sent.append((copy, when))

    def arrived(dst, r_sem):
        pltpu.make_async_copy(dst, dst, r_sem).wait()

    def piece(layer, col, q):
        return a_all.at[layer, col, pl.ds(q * size, size)]

    for k, one in enumerate(peers):
        send(am_ref, am_all.at[l, c], am_send.at[k], am_recv.at[l, c], one)
    for k, one in enumerate(sides):
        send(bm_ref, bm_all.at[l, i], bm_send.at[k], bm_recv.at[l, i], one)

    send(b_ref, b_all.at[l, i], b_send.at[0], b_recv.at[l, i], (i, c, m))
    for q in range(pieces):
        own = a_ref.at[pl.ds(q * size, size)]
        send(own, piece(l, c, q), up_sem.at[l, c, q], a_recv.at[l, c, q], (i, c + 1, l), c + 1 < n_col)
        send(own, piece(l, c, q), down_sem.at[l, c, q], a_recv.at[l, c, q], (i, c - 1, l), c >= 1)
        send(own, piece(l, c, q), over_sem.at[l, c, q], a_recv.at[l, c, q], (i, c, m))
    for dr in range(1, n_row):
        to = (lax.rem(i + dr, n_row), c, l)
        send(b_ref, b_all.at[l, i], b_send.at[dr], b_recv.at[l, i], to)
    mine = [
        pltpu.make_async_copy(a_ref, a_all.at[l, c], own_sem.at[0]),
        pltpu.make_async_copy(am_ref, am_all.at[l, c], own_sem.at[1]),
        pltpu.make_async_copy(b_ref, b_all.at[l, i], own_sem.at[2]),
        pltpu.make_async_copy(bm_ref, bm_all.at[l, i], own_sem.at[3]),
    ]
    for copy in mine:
        copy.start()

    arrived(b_all.at[m, i], b_recv.at[m, i])
    for dr in range(1, n_row):
        to = (lax.rem(i + dr, n_row), c, l)
        send(b_all.at[m, i], b_all.at[m, i], b_pass.at[dr], b_recv.at[m, i], to)

    for d in range(1, n_col):
        for q in range(pieces):
            low, high = c - d, c + d
            over_low = low >= 0
            over_high = high < n_col
            if d == 1 and short_cuts:
                over_low = (c >= 2) & (c < n_col - 1) if q < half else c >= 2
                over_high = (c >= 1) & (c < n_col - 2) if q < half else c < n_col - 2

            @pl.when(low >= 0)
            def _():
                arrived(piece(l, low, q), a_recv.at[l, low, q])

            part = piece(l, low, q)
            send(part, part, up_sem.at[l, low, q], a_recv.at[l, low, q], (i, c + 1, l),
                 (low >= 0) & (c + 1 < n_col))
            send(part, part, over_sem.at[l, low, q], a_recv.at[l, low, q], (i, c, m), over_low)

            @pl.when(high < n_col)
            def _():
                arrived(piece(l, high, q), a_recv.at[l, high, q])

            part = piece(l, high, q)
            send(part, part, down_sem.at[l, high, q], a_recv.at[l, high, q], (i, c - 1, l),
                 (high < n_col) & (c >= 1))
            send(part, part, over_sem.at[l, high, q], a_recv.at[l, high, q], (i, c, m), over_high)

            if d == 1:
                part = piece(m, c, q)
                arrived(part, a_recv.at[m, c, q])
                if short_cuts:
                    up = c == 0
                    down = c == n_col - 1
                    if q < half:
                        up = up | (c == n_col - 2)
                        down = down | (c == 1)
                    send(part, part, up_sem.at[m, c, q], a_recv.at[m, c, q], (i, c + 1, l), up)
                    send(part, part, down_sem.at[m, c, q], a_recv.at[m, c, q], (i, c - 1, l), down)

    for d in range(1, n_col):
        other = lax.rem(c + d, n_col)
        for q in range(pieces):
            arrived(piece(m, other, q), a_recv.at[m, other, q])
    for ll, cc in [(lax.rem(l + k // n_col, n_layer), lax.rem(c + k % n_col, n_col))
                   for k in range(1, n_layer * n_col)]:
        arrived(am_all.at[ll, cc], am_recv.at[ll, cc])
    for k in range(1, n_layer * n_row):
        ll, rr = lax.rem(l + k // n_row, n_layer), lax.rem(i + k % n_row, n_row)
        arrived(bm_all.at[ll, rr], bm_recv.at[ll, rr])
        if k != n_row:
            arrived(b_all.at[ll, rr], b_recv.at[ll, rr])
    for copy in mine:
        copy.wait()
    for copy, when in sent:
        if when is None:
            copy().wait_send()
        else:
            pl.when(when)(lambda copy=copy: copy().wait_send())


def gather(a, am, b, bm, n_row, n_col, n_layer):
    pieces = 4 if a.shape[0] % 4 == 0 else 1
    any_space = pl.BlockSpec(memory_space=pl.ANY)
    dma = pltpu.SemaphoreType.DMA
    return pl.pallas_call(
        functools.partial(gather_kernel, n_row, n_col, n_layer, pieces),
        out_shape=(
            jax.ShapeDtypeStruct((n_layer, n_col) + a.shape, a.dtype),
            jax.ShapeDtypeStruct((n_layer, n_col) + am.shape, am.dtype),
            jax.ShapeDtypeStruct((n_layer, n_row) + b.shape, b.dtype),
            jax.ShapeDtypeStruct((n_layer, n_row) + bm.shape, bm.dtype),
        ),
        in_specs=[any_space] * 4,
        out_specs=(any_space,) * 4,
        scratch_shapes=[
            dma((n_layer, n_col, pieces)),
            dma((n_layer, n_col, pieces)),
            dma((n_layer, n_col, pieces)),
            dma((n_layer, n_col, pieces)),
            dma((n_layer * n_col,)),
            dma((n_layer, n_col)),
            dma((n_row,)),
            dma((n_row,)),
            dma((n_layer, n_row)),
            dma((n_layer * n_row,)),
            dma((n_layer, n_row)),
            dma((4,)),
        ],
        compiler_params=pltpu.CompilerParams(collective_id=0, has_side_effects=True),
    )(a, am, b, bm)


def product_kernel(n_row, n_col, where, am, bm, a_ref, b_ref, out_ref, left, right):
    layer, turn = pl.program_id(0), pl.program_id(1)
    i, j, l = where[0], where[1], where[2]
    block = a_ref.shape[-1]
    width = out_ref.shape[1] // block
    group = lax.rem(i + turn, n_col)
    stack = group // n_row
    source = lax.rem(lax.rem(group, n_row) - lax.rem(j, n_row) + n_row, n_row)

    @pl.when((layer == 0) & (turn == 0))
    def _():
        out_ref[...] = jnp.zeros_like(out_ref)

    left[...] = jnp.zeros_like(left)
    right[...] = jnp.zeros_like(right)
    for s in range(a_ref.shape[2]):
        p = am[layer, turn, 0, s]

        @pl.when(p >= 0)
        def _():
            r = pl.multiple_of(p // KB * block, block)
            k = pl.multiple_of(lax.rem(p, KB) * block, block)
            left[pl.ds(r, block), pl.ds(k, block)] = a_ref[0, 0, s]

    for s in range(b_ref.shape[3]):
        p = bm[layer, source, 0, stack * b_ref.shape[3] + s]
        col = lax.rem(p, CB) - l * width

        @pl.when((p >= 0) & (col >= 0) & (col < width))
        def _():
            r = pl.multiple_of(p // CB * block, block)
            k = pl.multiple_of(col * block, block)
            right[pl.ds(r, block), pl.ds(k, block)] = b_ref[layer, source, stack, s]

    out_ref[...] += jnp.dot(left[...], right[...], preferred_element_type=jnp.float32)


def product(where, a_all, am, b_all, bm, n_row, n_col, n_layer):
    block = a_all.shape[-1]
    width = CB * block // n_layer
    return pl.pallas_call(
        functools.partial(product_kernel, n_row, n_col),
        out_shape=jax.ShapeDtypeStruct((RB * block, width), jnp.float32),
        grid_spec=pltpu.PrefetchScalarGridSpec(
            num_scalar_prefetch=3,
            grid=(n_layer, n_col),
            in_specs=[
                pl.BlockSpec((1, 1) + a_all.shape[2:], lambda g, t, *_: (g, t, 0, 0, 0)),
                pl.BlockSpec(memory_space=pltpu.VMEM),
            ],
            out_specs=pl.BlockSpec((RB * block, width), lambda g, t, *_: (0, 0)),
            scratch_shapes=[
                pltpu.VMEM((RB * block, KB * block), jnp.bfloat16),
                pltpu.VMEM((KB * block, width), jnp.bfloat16),
            ],
        ),
        compiler_params=pltpu.CompilerParams(vmem_limit_bytes=40 * 1024 * 1024),
    )(where, am, bm, a_all, b_all)


def masked(pos, count):
    slots = jnp.arange(pos.shape[-1], dtype=jnp.int32)
    flat = jnp.where(slots < count[..., None], pos, -1).reshape(1, -1)
    return jnp.pad(flat, ((0, 0), (0, 128 - flat.shape[1])), constant_values=-1)


def per_device(a_vals, a_pos, a_count, b_vals, b_pos, b_count):
    n_row = lax.axis_size("row")
    n_col = lax.axis_size("col")
    n_layer = lax.axis_size("layer")
    where = jnp.stack([lax.axis_index(name) for name in ("row", "col", "layer")]).astype(jnp.int32)
    am = masked(a_pos[0, 0, 0], a_count[0, 0, 0])
    bm = masked(b_pos[0, 0, 0], b_count[0, 0, 0])
    a_all, am_all, b_all, bm_all = gather(
        a_vals[0, 0, 0], am, b_vals[0, 0, 0], bm, n_row, n_col, n_layer)
    return product(where, a_all, am_all, b_all, bm_all, n_row, n_col, n_layer)


def solution(mesh):
    placed = (
        P("row", "col", "layer", None, None, None),
        P("row", "col", "layer", None),
        P("row", "col", "layer"),
        P("row", "col", "layer", None, None, None, None),
        P("row", "col", "layer", None, None),
        P("row", "col", "layer", None),
    )
    return jax.shard_map(
        per_device,
        mesh=mesh,
        in_specs=placed,
        out_specs=P("row", ("col", "layer")),
        check_vma=False,
    )
```

time: 267 us -> 95.9 us (0.36)
  Pallas kernels: 0 us -> 86.5 us
  starting transfers between devices: 65.7 us -> 0 us
  waiting for transfers between devices: 58.8 us -> 0 us
  matrix products: 52.3 us -> 0 us
  loops' own time: 49.3 us -> 0 us
  between operations: 30.3 us -> 1.32 us
    pallas_call x0 -> x2, Pallas kernels: none -> 86.5 us  [the longest x1 73.9 us: gather(): pl.pallas_call(functools.partial(gather_kernel, n_row, n_col, n_layer, pi...]
    ppermute x18 -> x0, starting transfers between devices: 65.7 us -> none  [passed_along(): return lax.ppermute(block, axis, route)]
    reduce_scatter x1 -> x0, waiting for transfers between devices: 54.9 us -> none  [per_device(): return lax.psum_scatter(total, 'layer', scatter_dimension=1, tiled=True)]
    dot_general x28 -> x0, matrix products: 52.3 us -> none  [the longest x24 50.1 us: contribute(): term = jnp.dot(left, b_vals[slot], preferred_element_type=jnp.float32)]
    another operation x1 -> x0, loops' own time: 49.3 us -> none  [per_device(): lax.fori_loop(0, n_col - 1, advance, (start, tuple(a_state), tuple(b_stat...]
    ppermute x18 -> x0, waiting for transfers between devices: 3.91 us -> none  [passed_along(): return lax.ppermute(block, axis, route)]
    unnamed x7 -> x8, local copies, waits for them, and re-layouts: 1.69 us -> 5.54 us
    slice x4 -> x0, local copies, waits for them, and re-layouts: 2.71 us -> none  [contribute(): entry = b_pos[slot]]
  transfers between devices with their start and end apart: 19 -> 0, of which waited for: 4 -> 0; matrix products, arithmetic and copies ran while one was open for 16% -> 0% of each run, Pallas kernels for 0% -> 0%
where the time goes in v1:
time: 95.9 us; the launch traced here: 95.8 us
  Pallas kernels  86.5 us (90%)
  local copies, waits for them, and re-layouts  6.64 us (7%)
  other arithmetic  1.4 us (1%)
  between operations  1.32 us (1%)
    pallas_call x1, Pallas kernels, gather(): pl.pallas_call(functools.partial(gather_kernel, n_row, n_col, n_layer, pi...  73.9 us
    pallas_call x1, Pallas kernels, product(): pl.pallas_call(functools.partial(product_kernel, n_row, n_col), out_shape...  12.6 us
    unnamed x8, local copies, waits for them, and re-layouts  5.54 us

profile of v1, /device:TPU:0, one launch (start us, length us, event | category | flops | bytes accessed | tf_op | source)
XLA Modules:
  0.0 95.8 jit_solution(12816698912885896491)
XLA Ops:
  1.3 0.1 pad_add_fusion.where
  1.4 0.7 compare_select_fusion
  2.0 0.6 pad.9.bm_ref
  2.6 0.7 compare_select_fusion.1
  3.3 0.5 pad.8.am_ref
  3.8 73.9 %shard_map.64 = (bf16[2,4,24,128,128]{4,3,2,1,0:T(8,128)(2,1)}, s32[2,4,1,128]{3,2,1,0:T(1,128)}, bf16[2,4,1,6,128,128]{5,4,3,2,1,0:T(8,128)(2,1)}, s32[2,4,1,128]{3,2,1,0:T(1,128)}) custom-call(bf16[24,128,128]{2,1,0:T(8,128)(2,1)} %bitcast.13, s32[1,128]{1,0:T(1,128)} %pad.8.am_ref, bf16[1,6,128,128]{3,2,1,0:T(8,128)(2,1)} %bitcast.14, s32[1,128]{1,0:T(1,128)} %pad.9.bm_ref), custom_call_target="tpu_custom_call" | custom-call | tf_op jit(solution)/shard_map/pallas_call | solution.py:162
  77.7 0.0 copy-start
  77.7 2.8 %copy-done = bf16[2,4,24,128,128]{4,3,2,1,0:T(8,128)(2,1)S(1)} copy-done((bf16[2,4,24,128,128]{4,3,2,1,0:T(8,128)(2,1)S(1)}, bf16[2,4,24,128,128]{4,3,2,1,0:T(8,128)(2,1)}, u32[]{:S(2)}) %copy-start) | copy-done | bytes 6291480
  80.5 0.0 copy-start.1
  80.5 1.4 %copy-done.1 = bf16[2,4,1,6,128,128]{5,4,3,2,1,0:T(8,128)(2,1)S(1)} copy-done((bf16[2,4,1,6,128,128]{5,4,3,2,1,0:T(8,128)(2,1)S(1)}, bf16[2,4,1,6,128,128]{5,4,3,2,1,0:T(8,128)(2,1)}, u32[]{:S(2)}) %copy-start.1) | copy-done | bytes 1572888
  81.9 0.0 copy-start.2
  81.9 0.7 copy-done.2
  82.5 0.0 copy-start.3
  82.5 0.7 copy-done.3
  83.2 12.6 %shard_map.65 = f32[1024,512]{1,0:T(8,128)} custom-call(s32[3]{0:T(128)S(1)} %pad_add_fusion.where, s32[2,4,1,128]{3,2,1,0:T(1,128)S(1)} %copy-done.2, s32[2,4,1,128]{3,2,1,0:T(1,128)S(1)} %copy-done.3, bf16[2,4,24,128,128]{4,3,2,1,0:T(8,128)(2,1)S(1)} %copy-done, bf16[2,4,1,6,128,128]{5,4,3,2,1,0:T(8,128)(2,1)S(1)} %copy-done.1), custom_call_target="tpu_custom_call" | custom-call | tf_op jit(solution)/shard_map/pallas_call | solution.py:230
Async XLA Ops:
  77.7 2.8 %copy-start = (bf16[2,4,24,128,128]{4,3,2,1,0:T(8,128)(2,1)S(1)}, bf16[2,4,24,128,128]{4,3,2,1,0:T(8,128)(2,1)}, u32[]{:S(2)}) copy-start(bf16[2,4,24,128,128]{4,3,2,1,0:T(8,128)(2,1)} %get-tuple-element.11.a_ref) | copy-start | bytes 18874372
  80.5 1.4 %copy-start.1 = (bf16[2,4,1,6,128,128]{5,4,3,2,1,0:T(8,128)(2,1)S(1)}, bf16[2,4,1,6,128,128]{5,4,3,2,1,0:T(8,128)(2,1)}, u32[]{:S(2)}) copy-start(bf16[2,4,1,6,128,128]{5,4,3,2,1,0:T(8,128)(2,1)} %get-tuple-element.12.b_ref) | copy-start | bytes 4718596
  81.9 0.7 copy-start.2
  82.5 0.7 copy-start.3

commit v2 on v0

v2 whole, which is shorter than its diff:
```python
import functools

import jax
import jax.numpy as jnp
from jax import lax
from jax.experimental import pallas as pl
from jax.experimental.pallas import tpu as pltpu
from jax.sharding import PartitionSpec as P

KB = 4
CB = 8
RB = 8
MESH = pl.DeviceIdType.MESH


def kernel(n_row, n_col, n_layer, pieces, a_ref, b_ref, map_ref, out_ref, *scratch):
    scratch = list(scratch)
    a_all = [[scratch.pop(0) for _ in range(n_col)] for _ in range(n_layer)]
    b_all = [[scratch.pop(0) for _ in range(n_row)] for _ in range(n_layer)]
    (a_maps, b_maps, a_places, b_places, left, right,
     up_sem, down_sem, over_sem, a_recv, am_send, am_recv,
     b_send, b_pass, b_recv, bm_send, bm_recv, own_sem) = scratch
    i = lax.axis_index("row")
    c = lax.axis_index("col")
    l = lax.axis_index("layer")
    m = 1 - l
    slots = a_ref.shape[0]
    slots_b = b_ref.shape[0]
    block = a_ref.shape[-1]
    width = out_ref.shape[1] // block
    size = slots // pieces
    half = pieces // 2
    short_cuts = n_col >= 4

    peers = [(dl, dc) for dl in range(n_layer) for dc in range(n_col) if dl or dc]
    sides = [(dl, dr) for dl in range(n_layer) for dr in range(n_row) if dl or dr]

    def peer(dl, dc):
        return (i, lax.rem(c + dc, n_col), lax.rem(l + dl, n_layer))

    def side(dl, dr):
        return (lax.rem(i + dr, n_row), c, lax.rem(l + dl, n_layer))

    barrier = pltpu.get_barrier_semaphore()
    greeted = [peer(*one) for one in peers] + [side(*one) for one in sides if one[1]]
    for one in greeted:
        pl.semaphore_signal(barrier, inc=1, device_id=one, device_id_type=MESH)
    mine = [
        pltpu.make_async_copy(a_ref, a_all[0][0].at[pl.ds(0, slots)], own_sem.at[0]),
        pltpu.make_async_copy(b_ref, b_all[0][0].at[pl.ds(0, slots_b)], own_sem.at[1]),
        pltpu.make_async_copy(map_ref, a_maps.at[0, 0], own_sem.at[2]),
        pltpu.make_async_copy(map_ref, b_maps.at[0, 0], own_sem.at[3]),
    ]
    for copy in mine:
        copy.start()
    for ref in [one for layer in a_all for one in layer]:
        ref[slots] = jnp.zeros((block, block), ref.dtype)
    for ref in [one for layer in b_all for one in layer]:
        ref[slots_b] = jnp.zeros((block, block), ref.dtype)
    pl.semaphore_wait(barrier, len(greeted))

    sent = []

    def send(src, dst, s_sem, r_sem, to, when=None):
        def copy():
            return pltpu.make_async_remote_copy(
                src_ref=src, dst_ref=dst, send_sem=s_sem, recv_sem=r_sem,
                device_id=to, device_id_type=MESH)

        if when is None:
            copy().start()
        else:
            pl.when(when)(lambda: copy().start())
        sent.append((copy, when))

    def arrived(dst, r_sem):
        pltpu.make_async_copy(dst, dst, r_sem).wait()

    def piece(dl, dc, q):
        return a_all[dl][dc].at[pl.ds(q * size, size)]

    def stored(dl, dr):
        return b_all[dl][dr].at[pl.ds(0, slots_b)]

    def back(dl, dc, n):
        return (n_layer - dl) % n_layer, (n - dc) % n

    for k, one in enumerate(peers):
        dl, dc = back(*one, n_col)
        send(map_ref, a_maps.at[dl, dc], am_send.at[k], am_recv.at[dl, dc], peer(*one))
    for k, one in enumerate(sides):
        dl, dr = back(*one, n_row)
        send(map_ref, b_maps.at[dl, dr], bm_send.at[k], bm_recv.at[dl, dr], side(*one))

    below, above, across = (i, c - 1, l), (i, c + 1, l), (i, c, m)
    send(b_ref, stored(1, 0), b_send.at[0], b_recv.at[1, 0], across)
    for q in range(pieces):
        own = a_ref.at[pl.ds(q * size, size)]
        send(own, piece(0, n_col - 1, q), up_sem.at[0, 0, q], a_recv.at[0, n_col - 1, q], above, c + 1 < n_col)
        send(own, piece(0, 1, q), down_sem.at[0, 0, q], a_recv.at[0, 1, q], below, c >= 1)
        send(own, piece(1, 0, q), over_sem.at[0, 0, q], a_recv.at[1, 0, q], across)
    for dr in range(1, n_row):
        send(b_ref, stored(0, n_row - dr), b_send.at[dr], b_recv.at[0, n_row - dr], side(0, dr))

    arrived(stored(1, 0), b_recv.at[1, 0])
    for dr in range(1, n_row):
        send(stored(1, 0), stored(1, n_row - dr), b_pass.at[dr], b_recv.at[1, n_row - dr], side(0, dr))

    for dl, dc in peers:
        arrived(a_maps.at[dl, dc], am_recv.at[dl, dc])
    for dl, dr in sides:
        arrived(b_maps.at[dl, dr], bm_recv.at[dl, dr])
    for copy in mine:
        copy.wait()
    tables = [
        pltpu.make_async_copy(a_maps, a_places, own_sem.at[4]),
        pltpu.make_async_copy(b_maps, b_places, own_sem.at[5]),
    ]
    for copy in tables:
        copy.start()
    for copy in tables:
        copy.wait()

    def multiply(dl, dc, first=False):
        dr = dc % n_row
        a, b = a_all[dl][dc], b_all[dl][dr]
        stack = lax.div(lax.rem(i + c + dc, n_col), n_row)
        base = RB * KB + stack * KB * CB + l * width
        for k in range(KB):
            for n in range(width):
                slot = b_places[dl, dr, 0, base + k * CB + n]
                right[k * block:(k + 1) * block, n * block:(n + 1) * block] = b[slot]
        for r in range(RB):
            for k in range(KB):
                slot = a_places[dl, dc, 0, r * KB + k]
                left[r * block:(r + 1) * block, k * block:(k + 1) * block] = a[slot]
        term = jnp.dot(left[...], right[...], preferred_element_type=jnp.float32)
        if first:
            out_ref[...] = term
        else:
            out_ref[...] += term

    def at_distance(d, dl):
        def low():
            multiply(dl, n_col - d)

        def high():
            multiply(dl, d)

        def low_wait():
            for q in range(pieces):
                arrived(piece(dl, n_col - d, q), a_recv.at[dl, n_col - d, q])

        def high_wait():
            for q in range(pieces):
                arrived(piece(dl, d, q), a_recv.at[dl, d, q])

        def one(condition, wait, body):
            def run():
                @pl.when(condition)
                def _():
                    if dl:
                        wait()
                    body()
            return run

        return [one(c >= d, low_wait, low), one(c + d < n_col, high_wait, high)]

    def gram():
        for dl, dr in sides:
            if (dl, dr) != (1, 0):
                arrived(stored(dl, dr), b_recv.at[dl, dr])

    todo = [lambda: multiply(0, 0, True)]
    for d in range(1, n_col):
        for q in range(pieces):
            low, high = n_col - d, d
            over_low = c >= d
            over_high = c + d < n_col
            if d == 1 and short_cuts:
                over_low = (c >= 2) & (c < n_col - 1) if q < half else c >= 2
                over_high = (c >= 1) & (c < n_col - 2) if q < half else c < n_col - 2

            @pl.when(c >= d)
            def _():
                arrived(piece(0, low, q), a_recv.at[0, low, q])

            part = piece(0, low, q)
            if low > 1:
                send(part, piece(0, low - 1, q), up_sem.at[0, low, q], a_recv.at[0, low - 1, q], above,
                     (c >= d) & (c + 1 < n_col))
            send(part, piece(1, low, q), over_sem.at[0, low, q], a_recv.at[1, low, q], across, over_low)

            @pl.when(c + d < n_col)
            def _():
                arrived(piece(0, high, q), a_recv.at[0, high, q])

            part = piece(0, high, q)
            if high + 1 < n_col:
                send(part, piece(0, high + 1, q), down_sem.at[0, high, q], a_recv.at[0, high + 1, q], below,
                     (c + d < n_col) & (c >= 1))
            send(part, piece(1, high, q), over_sem.at[1, high, q], a_recv.at[1, high, q], across, over_high)

            if d == 1:
                part = piece(1, 0, q)
                arrived(part, a_recv.at[1, 0, q])
                if short_cuts:
                    up = c == 0
                    down = c == n_col - 1
                    if q < half:
                        up = up | (c == n_col - 2)
                        down = down | (c == 1)
                    send(part, piece(1, n_col - 1, q), up_sem.at[1, 0, q], a_recv.at[1, n_col - 1, q], above, up)
                    send(part, piece(1, 1, q), down_sem.at[1, 0, q], a_recv.at[1, 1, q], below, down)
            if todo:
                todo.pop(0)()
        while todo:
            todo.pop(0)()
        todo = at_distance(d, 0)
        if d == 1:
            todo = [gram] + todo + [lambda: multiply(1, 0)]
        else:
            todo = todo + at_distance(d - 1, 1)
    todo = todo + at_distance(n_col - 1, 1)
    for one in todo:
        one()
    for copy, when in sent:
        if when is None:
            copy().wait_send()
        else:
            pl.when(when)(lambda copy=copy: copy().wait_send())


def place_map(pos, count, places):
    slots = pos.shape[-1]
    order = jnp.arange(slots, dtype=jnp.int32)
    free = jnp.where(order < count, pos, -1)
    hit = free[:, None] == jnp.arange(places, dtype=jnp.int32)[None, :]
    return jnp.min(jnp.where(hit, order[:, None], slots), axis=0)


def per_device(a_vals, a_pos, a_count, b_vals, b_pos, b_count):
    n_row = lax.axis_size("row")
    n_col = lax.axis_size("col")
    n_layer = lax.axis_size("layer")
    a = a_vals[0, 0, 0]
    stacks, slots_b = b_pos.shape[-2:]
    block = a.shape[-1]
    b = b_vals[0, 0, 0].reshape(stacks * slots_b, block, block)
    rows = [place_map(a_pos[0, 0, 0], a_count[0, 0, 0], RB * KB)]
    for h in range(stacks):
        one = place_map(b_pos[0, 0, 0, h], b_count[0, 0, 0, h], KB * CB)
        rows.append(jnp.where(one == slots_b, stacks * slots_b, one + h * slots_b))
    places = jnp.concatenate(rows)
    places = jnp.pad(places, (0, 128 - places.shape[0]))[None]
    pieces = 4 if a.shape[0] % 4 == 0 else 1
    width = CB * block // n_layer
    dma = pltpu.SemaphoreType.DMA
    any_space = pl.BlockSpec(memory_space=pl.ANY)
    maps = ((n_layer, n_col, 1, 128), (n_layer, n_row, 1, 128))
    return pl.pallas_call(
        functools.partial(kernel, n_row, n_col, n_layer, pieces),
        out_shape=jax.ShapeDtypeStruct((RB * block, width), jnp.float32),
        in_specs=[any_space] * 3,
        out_specs=pl.BlockSpec(memory_space=pltpu.VMEM),
        scratch_shapes=[pltpu.VMEM((a.shape[0] + 1, block, block), a.dtype)] * (n_layer * n_col)
        + [pltpu.VMEM((b.shape[0] + 1, block, block), b.dtype)] * (n_layer * n_row)
        + [
            pltpu.VMEM(maps[0], jnp.int32),
            pltpu.VMEM(maps[1], jnp.int32),
            pltpu.SMEM(maps[0], jnp.int32),
            pltpu.SMEM(maps[1], jnp.int32),
            pltpu.VMEM((RB * block, KB * block), a.dtype),
            pltpu.VMEM((KB * block, width), b.dtype),
            dma((n_layer, n_col, pieces)),
            dma((n_layer, n_col, pieces)),
            dma((n_layer, n_col, pieces)),
            dma((n_layer, n_col, pieces)),
            dma((n_layer * n_col,)),
            dma((n_layer, n_col)),
            dma((n_row,)),
            dma((n_row,)),
            dma((n_layer, n_row)),
            dma((n_layer * n_row,)),
            dma((n_layer, n_row)),
            dma((6,)),
        ],
        compiler_params=pltpu.CompilerParams(
            collective_id=0, has_side_effects=True, vmem_limit_bytes=52 * 1024 * 1024),
    )(a, b, places)


def solution(mesh):
    placed = (
        P("row", "col", "layer", None, None, None),
        P("row", "col", "layer", None),
        P("row", "col", "layer"),
        P("row", "col", "layer", None, None, None, None),
        P("row", "col", "layer", None, None),
        P("row", "col", "layer", None),
    )
    return jax.shard_map(
        per_device,
        mesh=mesh,
        in_specs=placed,
        out_specs=P("row", ("col", "layer")),
        check_vma=False,
    )
```

time: 267 us -> 83.6 us (0.31)
  Pallas kernels: 0 us -> 75.3 us
  starting transfers between devices: 65.7 us -> 0 us
  waiting for transfers between devices: 58.8 us -> 0 us
  matrix products: 52.3 us -> 0 us
  loops' own time: 49.3 us -> 0 us
  between operations: 30.3 us -> 1.31 us
  local copies, waits for them, and re-layouts: 8.81 us -> 5.15 us
    pallas_call x0 -> x1, Pallas kernels: none -> 75.3 us  [per_device(): pl.pallas_call(functools.partial(kernel, n_row, n_col, n_layer, pieces),...]
    ppermute x18 -> x0, starting transfers between devices: 65.7 us -> none  [passed_along(): return lax.ppermute(block, axis, route)]
    reduce_scatter x1 -> x0, waiting for transfers between devices: 54.9 us -> none  [per_device(): return lax.psum_scatter(total, 'layer', scatter_dimension=1, tiled=True)]
    dot_general x28 -> x0, matrix products: 52.3 us -> none  [the longest x24 50.1 us: contribute(): term = jnp.dot(left, b_vals[slot], preferred_element_type=jnp.float32)]
    another operation x1 -> x0, loops' own time: 49.3 us -> none  [per_device(): lax.fori_loop(0, n_col - 1, advance, (start, tuple(a_state), tuple(b_stat...]
    ppermute x18 -> x0, waiting for transfers between devices: 3.91 us -> none  [passed_along(): return lax.ppermute(block, axis, route)]
    unnamed x7 -> x5, local copies, waits for them, and re-layouts: 1.69 us -> 5.14 us
    slice x4 -> x0, local copies, waits for them, and re-layouts: 2.71 us -> none  [contribute(): entry = b_pos[slot]]
  transfers between devices with their start and end apart: 19 -> 0, of which waited for: 4 -> 0; matrix products, arithmetic and copies ran while one was open for 16% -> 0% of each run, Pallas kernels for 0% -> 0%
where the time goes in v2:
time: 83.6 us; the launch traced here: 83.3 us
  Pallas kernels  75.3 us (90%)
  local copies, waits for them, and re-layouts  5.15 us (6%)
  other arithmetic  1.58 us (2%)
  between operations  1.31 us (2%)
    pallas_call x1, Pallas kernels, per_device(): pl.pallas_call(functools.partial(kernel, n_row, n_col, n_layer, pieces),...  75.3 us
    unnamed x5, local copies, waits for them, and re-layouts  5.14 us

profile of v2, /device:TPU:0, one launch (start us, length us, event | category | flops | bytes accessed | tf_op | source)
XLA Modules:
  0.0 83.3 jit_solution(322211012226894609)
XLA Ops:
  1.3 0.7 compare_select_fusion.1
  2.0 0.1 select_reduce_fusion.1
  2.1 0.7 compare_select_fusion.2
  2.7 0.1 select_reduce_fusion
  2.8 0.1 pad_add_fusion
  2.9 0.0 copy-start
  2.9 1.1 %copy-done = bf16[1,1,1,24,128,128]{5,4,3,2,1,0:T(8,128)(2,1)S(1)} copy-done((bf16[1,1,1,24,128,128]{5,4,3,2,1,0:T(8,128)(2,1)S(1)}, bf16[1,1,1,24,128,128]{5,4,3,2,1,0:T(8,128)(2,1)}, u32[]{:S(2)}) %copy-start) | copy-done | bytes 786456
  4.0 0.0 copy-start.1
  4.0 0.9 %copy-done.1 = bf16[1,1,1,1,6,128,128]{6,5,4,3,2,1,0:T(8,128)(2,1)S(1)} copy-done((bf16[1,1,1,1,6,128,128]{6,5,4,3,2,1,0:T(8,128)(2,1)S(1)}, bf16[1,1,1,1,6,128,128]{6,5,4,3,2,1,0:T(8,128)(2,1)}, u32[]{:S(2)}) %copy-start.1) | copy-done | bytes 196632
  5.0 75.3 %shard_map.64 = f32[1024,512]{1,0:T(8,128)} custom-call(bf16[24,128,128]{2,1,0:T(8,128)(2,1)S(1)} %bitcast.12, bf16[6,128,128]{2,1,0:T(8,128)(2,1)S(1)} %bitcast.13, s32[1,128]{1,0:T(1,128)S(1)} %pad_bitcast_fusion.map_ref), custom_call_target="tpu_custom_call" | custom-call | tf_op jit(solution)/shard_map/pallas_call | solution.py:261
  80.2 3.1 %copy.10 = f32[1024,512]{1,0:T(8,128)} copy(f32[1024,512]{1,0:T(8,128)} %shard_map.64) | data formatting | bytes 4194304
  (2 shorter events, 0.0 us)
Async XLA Ops:
  2.9 1.1 %copy-start = (bf16[1,1,1,24,128,128]{5,4,3,2,1,0:T(8,128)(2,1)S(1)}, bf16[1,1,1,24,128,128]{5,4,3,2,1,0:T(8,128)(2,1)}, u32[]{:S(2)}) copy-start(bf16[1,1,1,24,128,128]{5,4,3,2,1,0:T(8,128)(2,1)} %param.6) | copy-start | bytes 2359300
  4.0 0.9 %copy-start.1 = (bf16[1,1,1,1,6,128,128]{6,5,4,3,2,1,0:T(8,128)(2,1)S(1)}, bf16[1,1,1,1,6,128,128]{6,5,4,3,2,1,0:T(8,128)(2,1)}, u32[]{:S(2)}) copy-start(bf16[1,1,1,1,6,128,128]{6,5,4,3,2,1,0:T(8,128)(2,1)} %param.9) | copy-start | bytes 589828

commit v3 on v2

--- a/solution.py
+++ b/solution.py
@@ -13,13 +13,14 @@
 MESH = pl.DeviceIdType.MESH
 
 
-def kernel(n_row, n_col, n_layer, pieces, a_ref, b_ref, map_ref, out_ref, *scratch):
+def kernel(n_row, n_col, n_layer, pieces,
+           a_ref, b_ref, a_pos, a_count, b_pos, b_count, out_ref, *scratch):
     scratch = list(scratch)
     a_all = [[scratch.pop(0) for _ in range(n_col)] for _ in range(n_layer)]
     b_all = [[scratch.pop(0) for _ in range(n_row)] for _ in range(n_layer)]
-    (a_maps, b_maps, a_places, b_places, left, right,
+    (a_maps, b_maps, a_places, b_places, a_pos_s, a_count_s, b_pos_s, b_count_s, left, right,
      up_sem, down_sem, over_sem, a_recv, am_send, am_recv,
-     b_send, b_pass, b_recv, bm_send, bm_recv, own_sem) = scratch
+     b_send, b_pass, b_recv, bm_send, bm_recv, own_sem, late_sem) = scratch
     i = lax.axis_index("row")
     c = lax.axis_index("col")
     l = lax.axis_index("layer")
@@ -29,7 +30,7 @@
     block = a_ref.shape[-1]
     width = out_ref.shape[1] // block
     size = slots // pieces
-    half = pieces // 2
+    half = (pieces * 5 + 4) // 8
     short_cuts = n_col >= 4
 
     peers = [(dl, dc) for dl in range(n_layer) for dc in range(n_col) if dl or dc]
@@ -48,15 +49,33 @@
     mine = [
         pltpu.make_async_copy(a_ref, a_all[0][0].at[pl.ds(0, slots)], own_sem.at[0]),
         pltpu.make_async_copy(b_ref, b_all[0][0].at[pl.ds(0, slots_b)], own_sem.at[1]),
-        pltpu.make_async_copy(map_ref, a_maps.at[0, 0], own_sem.at[2]),
-        pltpu.make_async_copy(map_ref, b_maps.at[0, 0], own_sem.at[3]),
     ]
-    for copy in mine:
+    small = [
+        pltpu.make_async_copy(a_pos, a_pos_s, own_sem.at[2]),
+        pltpu.make_async_copy(a_count, a_count_s, own_sem.at[3]),
+        pltpu.make_async_copy(b_pos, b_pos_s, own_sem.at[6]),
+        pltpu.make_async_copy(b_count, b_count_s, own_sem.at[7]),
+    ]
+    for copy in small + mine:
         copy.start()
     for ref in [one for layer in a_all for one in layer]:
         ref[slots] = jnp.zeros((block, block), ref.dtype)
     for ref in [one for layer in b_all for one in layer]:
         ref[slots_b] = jnp.zeros((block, block), ref.dtype)
+    for copy in small:
+        copy.wait()
+    lane = lax.broadcasted_iota(jnp.int32, (1, 128), 1)
+    places = jnp.where(lane < RB * KB, slots, slots_b)
+    for s in range(slots):
+        places = jnp.where((lane == a_pos_s[0, s]) & (s < a_count_s[0, 0]), s, places)
+    for h in range(b_pos_s.shape[0]):
+        start = RB * KB + h * KB * CB
+        for s in range(b_pos_s.shape[1]):
+            hit = (lane == start + b_pos_s[h, s]) & (s < b_count_s[0, h])
+            places = jnp.where(hit, h * b_pos_s.shape[1] + s, places)
+    a_maps[0, 0] = places
+    b_maps[0, 0] = places
+    map_ref = a_maps.at[0, 0]
     pl.semaphore_wait(barrier, len(greeted))
 
     sent = []
@@ -207,13 +226,15 @@
                 if short_cuts:
                     up = c == 0
                     down = c == n_col - 1
-                    if q < half:
-                        up = up | (c == n_col - 2)
-                        down = down | (c == 1)
                     send(part, piece(1, n_col - 1, q), up_sem.at[1, 0, q], a_recv.at[1, n_col - 1, q], above, up)
                     send(part, piece(1, 1, q), down_sem.at[1, 0, q], a_recv.at[1, 1, q], below, down)
             if todo:
                 todo.pop(0)()
+        if d == n_col - 2 and short_cuts:
+            for q in range(half):
+                part = piece(1, 0, q)
+                send(part, piece(1, n_col - 1, q), late_sem.at[0, q], a_recv.at[1, n_col - 1, q], above, c == n_col - 2)
+                send(part, piece(1, 1, q), late_sem.at[1, q], a_recv.at[1, 1, q], below, c == 1)
         while todo:
             todo.pop(0)()
         todo = at_distance(d, 0)
@@ -231,12 +252,20 @@
             pl.when(when)(lambda copy=copy: copy().wait_send())
 
 
-def place_map(pos, count, places):
-    slots = pos.shape[-1]
-    order = jnp.arange(slots, dtype=jnp.int32)
-    free = jnp.where(order < count, pos, -1)
-    hit = free[:, None] == jnp.arange(places, dtype=jnp.int32)[None, :]
-    return jnp.min(jnp.where(hit, order[:, None], slots), axis=0)
+def write_kernel(in_ref, out_ref):
+    out_ref[...] = in_ref[...]
+
+
+def write(total):
+    one = pl.BlockSpec((total.shape[0] // 4, total.shape[1]), lambda n: (n, 0))
+    return pl.pallas_call(
+        write_kernel,
+        out_shape=jax.ShapeDtypeStruct(total.shape, total.dtype),
+        grid=(4,),
+        in_specs=[one],
+        out_specs=one,
+        compiler_params=pltpu.CompilerParams(vmem_limit_bytes=63 * 1024 * 1024),
+    )(total)
 
 
 def per_device(a_vals, a_pos, a_count, b_vals, b_pos, b_count):
@@ -247,21 +276,17 @@
     stacks, slots_b = b_pos.shape[-2:]
     block = a.shape[-1]
     b = b_vals[0, 0, 0].reshape(stacks * slots_b, block, block)
-    rows = [place_map(a_pos[0, 0, 0], a_count[0, 0, 0], RB * KB)]
-    for h in range(stacks):
-        one = place_map(b_pos[0, 0, 0, h], b_count[0, 0, 0, h], KB * CB)
-        rows.append(jnp.where(one == slots_b, stacks * slots_b, one + h * slots_b))
-    places = jnp.concatenate(rows)
-    places = jnp.pad(places, (0, 128 - places.shape[0]))[None]
-    pieces = 4 if a.shape[0] % 4 == 0 else 1
+    pieces = max(1, 32 // n_col)
+    if a.shape[0] % pieces:
+        pieces = 1
     width = CB * block // n_layer
     dma = pltpu.SemaphoreType.DMA
-    any_space = pl.BlockSpec(memory_space=pl.ANY)
+    in_hbm = pl.BlockSpec(memory_space=pltpu.HBM)
     maps = ((n_layer, n_col, 1, 128), (n_layer, n_row, 1, 128))
-    return pl.pallas_call(
+    total = pl.pallas_call(
         functools.partial(kernel, n_row, n_col, n_layer, pieces),
         out_shape=jax.ShapeDtypeStruct((RB * block, width), jnp.float32),
-        in_specs=[any_space] * 3,
+        in_specs=[in_hbm] * 6,
         out_specs=pl.BlockSpec(memory_space=pltpu.VMEM),
         scratch_shapes=[pltpu.VMEM((a.shape[0] + 1, block, block), a.dtype)] * (n_layer * n_col)
         + [pltpu.VMEM((b.shape[0] + 1, block, block), b.dtype)] * (n_layer * n_row)
@@ -270,6 +295,10 @@
             pltpu.VMEM(maps[1], jnp.int32),
             pltpu.SMEM(maps[0], jnp.int32),
             pltpu.SMEM(maps[1], jnp.int32),
+            pltpu.SMEM((1, a_pos.shape[-1]), jnp.int32),
+            pltpu.SMEM((1, 1), jnp.int32),
+            pltpu.SMEM((stacks, slots_b), jnp.int32),
+            pltpu.SMEM((1, stacks), jnp.int32),
             pltpu.VMEM((RB * block, KB * block), a.dtype),
             pltpu.VMEM((KB * block, width), b.dtype),
             dma((n_layer, n_col, pieces)),
@@ -283,11 +312,13 @@
             dma((n_layer, n_row)),
             dma((n_layer * n_row,)),
             dma((n_layer, n_row)),
-            dma((6,)),
+            dma((8,)),
+            dma((2, pieces)),
         ],
         compiler_params=pltpu.CompilerParams(
-            collective_id=0, has_side_effects=True, vmem_limit_bytes=52 * 1024 * 1024),
-    )(a, b, places)
+            collective_id=0, has_side_effects=True, vmem_limit_bytes=63 * 1024 * 1024),
+    )(a, b, a_pos[0, 0], a_count[0], b_pos[0, 0, 0], b_count[0, 0])
+    return write(total)
 
 
 def solution(mesh):

time: 83.6 us -> 88.7 us (1.061)
  Pallas kernels: 75.3 us -> 87.2 us
  local copies, waits for them, and re-layouts: 5.15 us -> 0 us
  other arithmetic: 1.58 us -> 0 us
    pallas_call x1, Pallas kernels: 75.3 us -> 83.4 us  [per_device(): pl.pallas_call(functools.partial(kernel, n_row, n_col, n_layer, pieces),...]
    unnamed x5 -> x0, local copies, waits for them, and re-layouts: 5.14 us -> none
    pallas_call x0 -> x1, Pallas kernels: none -> 3.78 us  [write(): pl.pallas_call(write_kernel, out_shape=jax.ShapeDtypeStruct(total.shape,...]
    select_n x3 -> x0, other arithmetic: 1.33 us -> none  [the longest x2 1.32 us: place_map(): free = jnp.where(order < count, pos, -1)]
where the time goes in v3:
time: 88.7 us; the launch traced here: 88.5 us
  Pallas kernels  87.2 us (98%)
  between operations  1.3 us (1%)
    pallas_call x1, Pallas kernels, per_device(): pl.pallas_call(functools.partial(kernel, n_row, n_col, n_layer, pieces),...  83.4 us
    pallas_call x1, Pallas kernels, write(): pl.pallas_call(write_kernel, out_shape=jax.ShapeDtypeStruct(total.shape,...  3.78 us

profile of v3, /device:TPU:0, one launch (start us, length us, event | category | flops | bytes accessed | tf_op | source)
XLA Modules:
  0.0 88.5 jit_solution(13894814495592824724)
XLA Ops:
  1.3 83.4 %shard_map.64.in_ref = f32[1024,512]{1,0:T(8,128)} custom-call(bf16[24,128,128]{2,1,0:T(8,128)(2,1)} %bitcast.8, bf16[6,128,128]{2,1,0:T(8,128)(2,1)} %bitcast.9, s32[1,24]{1,0:T(1,128)} %bitcast.10, s32[1,1]{1,0:T(1,128)} %bitcast.6.a_count, s32[1,6]{1,0:T(1,128)} %bitcast.11, s32[1,1]{1,0:T(1,128)} %bitcast.7.b_count), custom_call_target="tpu_custom_call" | custom-call | tf_op jit(solution)/shard_map/pallas_call | solution.py:286
  84.7 3.8 %shard_map.65 = f32[1024,512]{1,0:T(8,128)} custom-call(f32[1024,512]{1,0:T(8,128)} %shard_map.64.in_ref), custom_call_target="tpu_custom_call" | custom-call | tf_op jit(solution)/shard_map/pallas_call | solution.py:261

commit v4 on v3

--- a/solution.py
+++ b/solution.py
@@ -10,6 +10,7 @@
 KB = 4
 CB = 8
 RB = 8
+IN_FLIGHT = 2
 MESH = pl.DeviceIdType.MESH
 
 
@@ -80,17 +81,28 @@
 
     sent = []
 
-    def send(src, dst, s_sem, r_sem, to, when=None):
+    streams = {}
+
+    def finish(copy, when):
+        if when is None:
+            copy().wait_send()
+        else:
+            pl.when(when)(lambda: copy().wait_send())
+
+    def send(src, dst, s_sem, r_sem, to, when=None, stream=None):
         def copy():
             return pltpu.make_async_remote_copy(
                 src_ref=src, dst_ref=dst, send_sem=s_sem, recv_sem=r_sem,
                 device_id=to, device_id_type=MESH)
 
+        flying = sent if stream is None else streams.setdefault(stream, [])
+        if stream is not None and len(flying) >= IN_FLIGHT:
+            finish(*flying.pop(0))
         if when is None:
             copy().start()
         else:
             pl.when(when)(lambda: copy().start())
-        sent.append((copy, when))
+        flying.append((copy, when))
 
     def arrived(dst, r_sem):
         pltpu.make_async_copy(dst, dst, r_sem).wait()
@@ -113,17 +125,17 @@
 
     below, above, across = (i, c - 1, l), (i, c + 1, l), (i, c, m)
     send(b_ref, stored(1, 0), b_send.at[0], b_recv.at[1, 0], across)
+    for dr in range(1, n_row):
+        send(b_ref, stored(0, n_row - dr), b_send.at[dr], b_recv.at[0, n_row - dr], side(0, dr))
     for q in range(pieces):
         own = a_ref.at[pl.ds(q * size, size)]
-        send(own, piece(0, n_col - 1, q), up_sem.at[0, 0, q], a_recv.at[0, n_col - 1, q], above, c + 1 < n_col)
-        send(own, piece(0, 1, q), down_sem.at[0, 0, q], a_recv.at[0, 1, q], below, c >= 1)
-        send(own, piece(1, 0, q), over_sem.at[0, 0, q], a_recv.at[1, 0, q], across)
-    for dr in range(1, n_row):
-        send(b_ref, stored(0, n_row - dr), b_send.at[dr], b_recv.at[0, n_row - dr], side(0, dr))
-
-    arrived(stored(1, 0), b_recv.at[1, 0])
-    for dr in range(1, n_row):
-        send(stored(1, 0), stored(1, n_row - dr), b_pass.at[dr], b_recv.at[1, n_row - dr], side(0, dr))
+        send(own, piece(0, n_col - 1, q), up_sem.at[0, 0, q], a_recv.at[0, n_col - 1, q], above, c + 1 < n_col, "up")
+        send(own, piece(0, 1, q), down_sem.at[0, 0, q], a_recv.at[0, 1, q], below, c >= 1, "down")
+        send(own, piece(1, 0, q), over_sem.at[0, 0, q], a_recv.at[1, 0, q], across, None, "over")
+        if q == pieces // 2:
+            arrived(stored(1, 0), b_recv.at[1, 0])
+            for dr in range(1, n_row):
+                send(stored(1, 0), stored(1, n_row - dr), b_pass.at[dr], b_recv.at[1, n_row - dr], side(0, dr))
 
     for dl, dc in peers:
         arrived(a_maps.at[dl, dc], am_recv.at[dl, dc])
@@ -185,10 +197,9 @@
 
         return [one(c >= d, low_wait, low), one(c + d < n_col, high_wait, high)]
 
-    def gram():
-        for dl, dr in sides:
-            if (dl, dr) != (1, 0):
-                arrived(stored(dl, dr), b_recv.at[dl, dr])
+    def gram(dl):
+        for dr in range(1, n_row):
+            arrived(stored(dl, dr), b_recv.at[dl, dr])
 
     todo = [lambda: multiply(0, 0, True)]
     for d in range(1, n_col):
@@ -207,8 +218,8 @@
             part = piece(0, low, q)
             if low > 1:
                 send(part, piece(0, low - 1, q), up_sem.at[0, low, q], a_recv.at[0, low - 1, q], above,
-                     (c >= d) & (c + 1 < n_col))
-            send(part, piece(1, low, q), over_sem.at[0, low, q], a_recv.at[1, low, q], across, over_low)
+                     (c >= d) & (c + 1 < n_col), "up")
+            send(part, piece(1, low, q), over_sem.at[0, low, q], a_recv.at[1, low, q], across, over_low, "over low")
 
             @pl.when(c + d < n_col)
             def _():
@@ -217,8 +228,8 @@
             part = piece(0, high, q)
             if high + 1 < n_col:
                 send(part, piece(0, high + 1, q), down_sem.at[0, high, q], a_recv.at[0, high + 1, q], below,
-                     (c + d < n_col) & (c >= 1))
-            send(part, piece(1, high, q), over_sem.at[1, high, q], a_recv.at[1, high, q], across, over_high)
+                     (c + d < n_col) & (c >= 1), "down")
+            send(part, piece(1, high, q), over_sem.at[1, high, q], a_recv.at[1, high, q], across, over_high, "over")
 
             if d == 1:
                 part = piece(1, 0, q)
@@ -226,46 +237,30 @@
                 if short_cuts:
                     up = c == 0
                     down = c == n_col - 1
-                    send(part, piece(1, n_col - 1, q), up_sem.at[1, 0, q], a_recv.at[1, n_col - 1, q], above, up)
-                    send(part, piece(1, 1, q), down_sem.at[1, 0, q], a_recv.at[1, 1, q], below, down)
+                    send(part, piece(1, n_col - 1, q), up_sem.at[1, 0, q], a_recv.at[1, n_col - 1, q], above, up, "turn up")
+                    send(part, piece(1, 1, q), down_sem.at[1, 0, q], a_recv.at[1, 1, q], below, down, "turn down")
             if todo:
                 todo.pop(0)()
         if d == n_col - 2 and short_cuts:
             for q in range(half):
                 part = piece(1, 0, q)
-                send(part, piece(1, n_col - 1, q), late_sem.at[0, q], a_recv.at[1, n_col - 1, q], above, c == n_col - 2)
-                send(part, piece(1, 1, q), late_sem.at[1, q], a_recv.at[1, 1, q], below, c == 1)
+                send(part, piece(1, n_col - 1, q), late_sem.at[0, q], a_recv.at[1, n_col - 1, q], above, c == n_col - 2, "up")
+                send(part, piece(1, 1, q), late_sem.at[1, q], a_recv.at[1, 1, q], below, c == 1, "down")
+                if todo:
+                    todo.pop(0)()
         while todo:
             todo.pop(0)()
         todo = at_distance(d, 0)
         if d == 1:
-            todo = [gram] + todo + [lambda: multiply(1, 0)]
+            todo = [lambda: gram(0)] + todo + [lambda: multiply(1, 0), lambda: gram(1)]
         else:
             todo = todo + at_distance(d - 1, 1)
     todo = todo + at_distance(n_col - 1, 1)
     for one in todo:
         one()
-    for copy, when in sent:
-        if when is None:
-            copy().wait_send()
-        else:
-            pl.when(when)(lambda copy=copy: copy().wait_send())
-
-
-def write_kernel(in_ref, out_ref):
-    out_ref[...] = in_ref[...]
-
-
-def write(total):
-    one = pl.BlockSpec((total.shape[0] // 4, total.shape[1]), lambda n: (n, 0))
-    return pl.pallas_call(
-        write_kernel,
-        out_shape=jax.ShapeDtypeStruct(total.shape, total.dtype),
-        grid=(4,),
-        in_specs=[one],
-        out_specs=one,
-        compiler_params=pltpu.CompilerParams(vmem_limit_bytes=63 * 1024 * 1024),
-    )(total)
+    for flying in [sent] + list(streams.values()):
+        for one in flying:
+            finish(*one)
 
 
 def per_device(a_vals, a_pos, a_count, b_vals, b_pos, b_count):
@@ -318,7 +313,7 @@
         compiler_params=pltpu.CompilerParams(
             collective_id=0, has_side_effects=True, vmem_limit_bytes=63 * 1024 * 1024),
     )(a, b, a_pos[0, 0], a_count[0], b_pos[0, 0, 0], b_count[0, 0])
-    return write(total)
+    return total
 
 
 def solution(mesh):

time: 88.7 us -> 88.6 us (level)
  Pallas kernels: 87.2 us -> 84 us
  local copies, waits for them, and re-layouts: 0 us -> 3.08 us
    pallas_call x1 -> x0, Pallas kernels: 3.78 us -> none  [write(): pl.pallas_call(write_kernel, out_shape=jax.ShapeDtypeStruct(total.shape,...]
    unnamed x0 -> x1, local copies, waits for them, and re-layouts: none -> 3.08 us
where the time goes in v4:
time: 88.6 us; the launch traced here: 88.4 us
  Pallas kernels  84 us (95%)
  local copies, waits for them, and re-layouts  3.08 us (3%)
  between operations  1.3 us (1%)
    pallas_call x1, Pallas kernels, per_device(): pl.pallas_call(functools.partial(kernel, n_row, n_col, n_layer, pieces),...  84 us
    unnamed x1, local copies, waits for them, and re-layouts  3.08 us

profile of v4, /device:TPU:0, one launch (start us, length us, event | category | flops | bytes accessed | tf_op | source)
XLA Modules:
  0.0 88.4 jit_solution(3223739848427629470)
XLA Ops:
  1.3 84.0 %shard_map.64 = f32[1024,512]{1,0:T(8,128)} custom-call(bf16[24,128,128]{2,1,0:T(8,128)(2,1)} %bitcast.8, bf16[6,128,128]{2,1,0:T(8,128)(2,1)} %bitcast.9, s32[1,24]{1,0:T(1,128)} %bitcast.10, s32[1,1]{1,0:T(1,128)} %bitcast.6.a_count, s32[1,6]{1,0:T(1,128)} %bitcast.11, s32[1,1]{1,0:T(1,128)} %bitcast.7.b_count), custom_call_target="tpu_custom_call" | custom-call | tf_op jit(solution)/shard_map/pallas_call | solution.py:281
  85.3 3.1 %copy.10 = f32[1024,512]{1,0:T(8,128)} copy(f32[1024,512]{1,0:T(8,128)} %shard_map.64) | data formatting | bytes 4194304

commit v5 on v4

--- a/solution.py
+++ b/solution.py
@@ -10,7 +10,7 @@
 KB = 4
 CB = 8
 RB = 8
-IN_FLIGHT = 2
+IN_FLIGHT = 4
 MESH = pl.DeviceIdType.MESH
 
 
@@ -253,9 +253,10 @@
         todo = at_distance(d, 0)
         if d == 1:
             todo = [lambda: gram(0)] + todo + [lambda: multiply(1, 0), lambda: gram(1)]
-        else:
+        elif d > 2:
             todo = todo + at_distance(d - 1, 1)
-    todo = todo + at_distance(n_col - 1, 1)
+    for d in sorted({1, n_col - 1}):
+        todo = todo + at_distance(d, 1)
     for one in todo:
         one()
     for flying in [sent] + list(streams.values()):

time: 88.6 us -> 79 us (0.89)
  Pallas kernels: 84 us -> 74.5 us
    pallas_call x1, Pallas kernels: 84 us -> 74.5 us  [per_device(): pl.pallas_call(functools.partial(kernel, n_row, n_col, n_layer, pieces),...]
where the time goes in v5:
time: 79 us; the launch traced here: 78.8 us
  Pallas kernels  74.5 us (94%)
  local copies, waits for them, and re-layouts  3.08 us (4%)
  between operations  1.3 us (2%)
    pallas_call x1, Pallas kernels, per_device(): pl.pallas_call(functools.partial(kernel, n_row, n_col, n_layer, pieces),...  74.5 us
    unnamed x1, local copies, waits for them, and re-layouts  3.08 us

profile of v5, /device:TPU:0, one launch (start us, length us, event | category | flops | bytes accessed | tf_op | source)
XLA Modules:
  0.0 78.8 jit_solution(13380621921298493022)
XLA Ops:
  1.3 74.5 %shard_map.64 = f32[1024,512]{1,0:T(8,128)} custom-call(bf16[24,128,128]{2,1,0:T(8,128)(2,1)} %bitcast.8, bf16[6,128,128]{2,1,0:T(8,128)(2,1)} %bitcast.9, s32[1,24]{1,0:T(1,128)} %bitcast.10, s32[1,1]{1,0:T(1,128)} %bitcast.6.a_count, s32[1,6]{1,0:T(1,128)} %bitcast.11, s32[1,1]{1,0:T(1,128)} %bitcast.7.b_count), custom_call_target="tpu_custom_call" | custom-call | tf_op jit(solution)/shard_map/pallas_call | solution.py:282
  75.8 3.1 %copy.10 = f32[1024,512]{1,0:T(8,128)} copy(f32[1024,512]{1,0:T(8,128)} %shard_map.64) | data formatting | bytes 4194304

commit v6 on v5

--- a/solution.py
+++ b/solution.py
@@ -63,6 +63,57 @@
         ref[slots] = jnp.zeros((block, block), ref.dtype)
     for ref in [one for layer in b_all for one in layer]:
         ref[slots_b] = jnp.zeros((block, block), ref.dtype)
+    pl.semaphore_wait(barrier, len(greeted))
+
+    sent = []
+
+    streams = {}
+
+    def finish(copy, when):
+        if when is None:
+            copy().wait_send()
+        else:
+            pl.when(when)(lambda: copy().wait_send())
+
+    def send(src, dst, s_sem, r_sem, to, when=None, stream=None):
+        def copy():
+            return pltpu.make_async_remote_copy(
+                src_ref=src, dst_ref=dst, send_sem=s_sem, recv_sem=r_sem,
+                device_id=to, device_id_type=MESH)
+
+        flying = sent if stream is None else streams.setdefault(stream, [])
+        if stream is not None and len(flying) >= IN_FLIGHT:
+            finish(*flying.pop(0))
+        if when is None:
+            copy().start()
+        else:
+            pl.when(when)(lambda: copy().start())
+        flying.append((copy, when))
+
+    def arrived(dst, r_sem):
+        pltpu.make_async_copy(dst, dst, r_sem).wait()
+
+    def piece(dl, dc, q):
+        return a_all[dl][dc].at[pl.ds(q * size, size)]
+
+    def stored(dl, dr):
+        return b_all[dl][dr].at[pl.ds(0, slots_b)]
+
+    def back(dl, dc, n):
+        return (n_layer - dl) % n_layer, (n - dc) % n
+
+    below, above, across = (i, c - 1, l), (i, c + 1, l), (i, c, m)
+
+    def own_piece(q):
+        own = a_ref.at[pl.ds(q * size, size)]
+        send(own, piece(0, n_col - 1, q), up_sem.at[0, 0, q], a_recv.at[0, n_col - 1, q], above, c + 1 < n_col, "up")
+        send(own, piece(0, 1, q), down_sem.at[0, 0, q], a_recv.at[0, 1, q], below, c >= 1, "down")
+        send(own, piece(1, 0, q), over_sem.at[0, 0, q], a_recv.at[1, 0, q], across, None, "over")
+
+    first = min(IN_FLIGHT, pieces)
+    for q in range(first):
+        own_piece(q)
+    send(b_ref, stored(1, 0), b_send.at[0], b_recv.at[1, 0], across)
     for copy in small:
         copy.wait()
     lane = lax.broadcasted_iota(jnp.int32, (1, 128), 1)
@@ -77,45 +128,6 @@
     a_maps[0, 0] = places
     b_maps[0, 0] = places
     map_ref = a_maps.at[0, 0]
-    pl.semaphore_wait(barrier, len(greeted))
-
-    sent = []
-
-    streams = {}
-
-    def finish(copy, when):
-        if when is None:
-            copy().wait_send()
-        else:
-            pl.when(when)(lambda: copy().wait_send())
-
-    def send(src, dst, s_sem, r_sem, to, when=None, stream=None):
-        def copy():
-            return pltpu.make_async_remote_copy(
-                src_ref=src, dst_ref=dst, send_sem=s_sem, recv_sem=r_sem,
-                device_id=to, device_id_type=MESH)
-
-        flying = sent if stream is None else streams.setdefault(stream, [])
-        if stream is not None and len(flying) >= IN_FLIGHT:
-            finish(*flying.pop(0))
-        if when is None:
-            copy().start()
-        else:
-            pl.when(when)(lambda: copy().start())
-        flying.append((copy, when))
-
-    def arrived(dst, r_sem):
-        pltpu.make_async_copy(dst, dst, r_sem).wait()
-
-    def piece(dl, dc, q):
-        return a_all[dl][dc].at[pl.ds(q * size, size)]
-
-    def stored(dl, dr):
-        return b_all[dl][dr].at[pl.ds(0, slots_b)]
-
-    def back(dl, dc, n):
-        return (n_layer - dl) % n_layer, (n - dc) % n
-
     for k, one in enumerate(peers):
         dl, dc = back(*one, n_col)
         send(map_ref, a_maps.at[dl, dc], am_send.at[k], am_recv.at[dl, dc], peer(*one))
@@ -123,19 +135,13 @@
         dl, dr = back(*one, n_row)
         send(map_ref, b_maps.at[dl, dr], bm_send.at[k], bm_recv.at[dl, dr], side(*one))
 
-    below, above, across = (i, c - 1, l), (i, c + 1, l), (i, c, m)
-    send(b_ref, stored(1, 0), b_send.at[0], b_recv.at[1, 0], across)
     for dr in range(1, n_row):
         send(b_ref, stored(0, n_row - dr), b_send.at[dr], b_recv.at[0, n_row - dr], side(0, dr))
-    for q in range(pieces):
-        own = a_ref.at[pl.ds(q * size, size)]
-        send(own, piece(0, n_col - 1, q), up_sem.at[0, 0, q], a_recv.at[0, n_col - 1, q], above, c + 1 < n_col, "up")
-        send(own, piece(0, 1, q), down_sem.at[0, 0, q], a_recv.at[0, 1, q], below, c >= 1, "down")
-        send(own, piece(1, 0, q), over_sem.at[0, 0, q], a_recv.at[1, 0, q], across, None, "over")
-        if q == pieces // 2:
-            arrived(stored(1, 0), b_recv.at[1, 0])
-            for dr in range(1, n_row):
-                send(stored(1, 0), stored(1, n_row - dr), b_pass.at[dr], b_recv.at[1, n_row - dr], side(0, dr))
+    for q in range(first, pieces):
+        own_piece(q)
+    arrived(stored(1, 0), b_recv.at[1, 0])
+    for dr in range(1, n_row):
+        send(stored(1, 0), stored(1, n_row - dr), b_pass.at[dr], b_recv.at[1, n_row - dr], side(0, dr))
 
     for dl, dc in peers:
         arrived(a_maps.at[dl, dc], am_recv.at[dl, dc])

time: 79 us -> 79 us (level)
  no operation moved by 1% of the time
where the time goes in v6:
time: 79 us; the launch traced here: 78.8 us
  Pallas kernels  74.5 us (94%)
  local copies, waits for them, and re-layouts  3.08 us (4%)
  between operations  1.3 us (2%)
    pallas_call x1, Pallas kernels, per_device(): pl.pallas_call(functools.partial(kernel, n_row, n_col, n_layer, pieces),...  74.5 us
    unnamed x1, local copies, waits for them, and re-layouts  3.08 us

profile of v6, /device:TPU:0, one launch (start us, length us, event | category | flops | bytes accessed | tf_op | source)
XLA Modules:
  0.0 78.8 jit_solution(15216821025529621783)
XLA Ops:
  1.3 74.5 %shard_map.64 = f32[1024,512]{1,0:T(8,128)} custom-call(bf16[24,128,128]{2,1,0:T(8,128)(2,1)} %bitcast.8, bf16[6,128,128]{2,1,0:T(8,128)(2,1)} %bitcast.9, s32[1,24]{1,0:T(1,128)} %bitcast.10, s32[1,1]{1,0:T(1,128)} %bitcast.6.a_count, s32[1,6]{1,0:T(1,128)} %bitcast.11, s32[1,1]{1,0:T(1,128)} %bitcast.7.b_count), custom_call_target="tpu_custom_call" | custom-call | tf_op jit(solution)/shard_map/pallas_call | solution.py:288
  75.8 3.1 %copy.10 = f32[1024,512]{1,0:T(8,128)} copy(f32[1024,512]{1,0:T(8,128)} %shard_map.64) | data formatting | bytes 4194304
